TPU v7x, 32 devices: a whole 2x2x4 slice. The times are simulated.
32 devices in a mesh: grp: 2 (over y), blk: 4 (over z), sub: 2 (over x), lev: 2 (over core).
Axes of the slice: x: 2, y: 2, z: 4, core: 2. Of those that a mesh axis runs over, the one named last changes fastest.
Arguments:
- tracers: float32 [4, 20, 32, 16, 128], P('grp', 'lev', ('blk', 'sub')), parts along dimension 0, may hold values from -6 to 6
- horizontal_diffusivity: float32 [32, 16, 128], P(('blk', 'sub')), may hold values from 0.03 to 0.12
- vertical_mixing: float32 [19], replicated, may hold values from 0.02 to 0.2
- layer_thickness: float32 [20], replicated, may hold values from 0.1 to 0.4
- surface_diagonal: float32 [32, 16, 128], P(('blk', 'sub')), may hold values from 0.3 to 3
- neighbours: int32 [32, 4], P(('blk', 'sub')), may hold values from -1 to 31, as said below
- baro_blocks: int32 [48], P(('blk', 'sub', 'lev')), may hold values from -1 to 31, as said below
Outputs:
- tracer_next: float32 [4, 20, 32, 16, 128], P('grp', 'lev', ('blk', 'sub')), parts along dimension 0
- pressure: float32 [40, 32, 16, 128], P(('grp', 'lev'), ('blk', 'sub')), parts along dimension 0
- surface_height: float32 [96, 16, 128], P(('grp', 'blk', 'sub', 'lev')), parts along dimension 0
There are 2 independent parts, one for each index of `grp`. A program takes and returns all parts, laid end to end along the dimension named above; an argument that names none is the same for every part. Nothing has to cross between parts.
Inputs may be any that keep to these rules, and one draw needn't show every extreme that they name: Blocks lie on a grid of 12 x 4 block places of which a third are land; ocean blocks are ranked in order along a curve that runs along each block row, alternately left to right and right to left. neighbours[q, s] is the rank of the ocean block beside q on side s (0 previous row, 1 next row, 2 previous column, 3 next column), or -1 for land or the grid's edge; the relation is symmetric, and a neighbour's rank lies in the same or an adjacent run of 8 ranks starting at a multiple of 8. `baro_blocks`: each surface owner (in the order blk, sub, lev) holds a run of consecutive ranks in its first slots and -1 in the rest; the runs follow one another and cover all ranks, those of one blk index b covering ranks 8 * b to 8 * b + 7. In each blk index one owner holds 3 ranks, one owner beside it within that index holds a quarter of 4, and all others half of 4.
All inputs are finite; a program needn't handle non-finite values.
Results may differ from a plain program's by a relative error of at most 0.0001.
Values sent between devices are 32-bit elements; how exact they have to be, the bound alone decides.
A program may use at most 64 MiB of HBM per device.

v0:
```python
import jax
import jax.numpy as jnp
from jax import lax
from jax.sharding import PartitionSpec as P

ITERS = 3


def passed_along(block, axis, distance):
    devices = range(lax.axis_size(axis))
    route = [(i - distance, i) for i in devices if i - distance in devices]
    return lax.ppermute(block, axis, route)


def with_halo(block, sides, width):
    for axis, dim in sides:
        count = lax.axis_size(axis)
        forward = [(i, i + 1) for i in range(count - 1)]
        backward = [(target, source) for source, target in forward]
        low = lax.ppermute(
            lax.slice_in_dim(block, block.shape[dim] - width, None, axis=dim), axis, forward
        )
        high = lax.ppermute(lax.slice_in_dim(block, 0, width, axis=dim), axis, backward)
        block = jnp.concatenate([low, block, high], axis=dim)
    return block


def prefix_2(value, axis, join, neutral):
    count, mine = (lax.axis_size(axis), lax.axis_index(axis))
    pieces = lax.all_gather(value, axis)
    total = jnp.full_like(value, 0) + jnp.asarray(neutral, value.dtype)

    def step(position, total):
        longer = join(total, pieces[position])
        return jnp.where(position < mine, longer, total)

    return lax.fori_loop(0, count - 1, step, total)


def edge_strips(values):
    return jnp.concatenate(
        [values[..., 0, :], values[..., -1, :], values[..., :, 0], values[..., :, -1]], axis=-1
    )


def pick_halos(gathered, row_count, col_count):
    halo_above = gathered[..., 0, col_count : 2 * col_count]
    halo_below = gathered[..., 1, 0:col_count]
    halo_west = gathered[..., 2, 2 * col_count + row_count : 2 * col_count + 2 * row_count]
    halo_east = gathered[..., 3, 2 * col_count : 2 * col_count + row_count]
    return (halo_above, halo_below, halo_west, halo_east)


def spread_sum(values, halos, opened):
    row_count, col_count = (values.shape[-2], values.shape[-1])
    halo_above, halo_below, halo_west, halo_east = halos
    from_above = jnp.concatenate([halo_above[..., None, :], values[..., :-1, :]], axis=-2)
    from_below = jnp.concatenate([values[..., 1:, :], halo_below[..., None, :]], axis=-2)
    from_west = jnp.concatenate([halo_west[..., :, None], values[..., :, :-1]], axis=-1)
    from_east = jnp.concatenate([values[..., :, 1:], halo_east[..., :, None]], axis=-1)
    row_ids = lax.broadcasted_iota(jnp.int32, (row_count, col_count), 0)
    col_ids = lax.broadcasted_iota(jnp.int32, (row_count, col_count), 1)
    unity = jnp.ones((row_count, col_count), jnp.float32)
    open_up = jnp.where(row_ids == 0, opened[:, 0, None, None], unity)
    open_down = jnp.where(row_ids == row_count - 1, opened[:, 1, None, None], unity)
    open_west = jnp.where(col_ids == 0, opened[:, 2, None, None], unity)
    open_east = jnp.where(col_ids == col_count - 1, opened[:, 3, None, None], unity)
    return (
        open_up * (from_above - values)
        + open_down * (from_below - values)
        + open_west * (from_west - values)
        + open_east * (from_east - values)
    )


def clinic_window(strips):
    together = lax.all_gather(strips, "sub", axis=2, tiled=True)
    from_lower = passed_along(together, "blk", 1)
    from_upper = passed_along(together, "blk", -1)
    return jnp.concatenate([from_lower, together, from_upper], axis=2)


def tropic_window(values):
    together = lax.all_gather(values, ("sub", "lev"), axis=0, tiled=True)
    from_lower = passed_along(together, "blk", 1)
    from_upper = passed_along(together, "blk", -1)
    return jnp.concatenate([from_lower, together, from_upper], axis=0)


def find_places(window_ranks, wanted):
    matched = window_ranks[None, :] == wanted[:, None]
    places = lax.broadcasted_iota(jnp.int32, matched.shape, 1)
    return jnp.clip(jnp.sum(jnp.where(matched, places, 0), axis=1), 0, window_ranks.shape[0] - 1)


def local(
    tracers,
    horizontal_diffusivity,
    vertical_mixing,
    layer_thickness,
    surface_diagonal,
    neighbours,
    baro_blocks,
):
    levels_here = tracers.shape[1]
    owned_blocks = tracers.shape[2]
    row_count, col_count = (tracers.shape[3], tracers.shape[4])
    group_size = owned_blocks * lax.axis_size("sub")
    peer_count = lax.axis_size("sub") * lax.axis_size("lev")
    slot_count = baro_blocks.shape[0]
    lev_index = lax.axis_index("lev")
    blk_index = lax.axis_index("blk")
    sub_index = lax.axis_index("sub")
    group_base = blk_index * group_size
    first_level = lev_index * levels_here
    end_levels = jnp.concatenate([tracers[:, :1], tracers[:, -1:]], axis=1)
    padded_ends = with_halo(end_levels, (("lev", 1),), 1)
    shallower = jnp.concatenate([padded_ends[:, :1], tracers[:, :-1]], axis=1)
    deeper = jnp.concatenate([tracers[:, 1:], padded_ends[:, 3:]], axis=1)
    boundary_zero = jnp.zeros((1,), jnp.float32)
    mixing_pad = jnp.concatenate([boundary_zero, vertical_mixing, boundary_zero])
    rate_above = lax.dynamic_slice_in_dim(mixing_pad, first_level, levels_here).reshape(
        1, levels_here, 1, 1, 1
    )
    rate_below = lax.dynamic_slice_in_dim(mixing_pad, first_level + 1, levels_here).reshape(
        1, levels_here, 1, 1, 1
    )
    vertical = rate_below * (deeper - tracers) - rate_above * (tracers - shallower)
    window = clinic_window(edge_strips(tracers))
    local_index = jnp.clip(neighbours - (blk_index - 1) * group_size, 0, 3 * group_size - 1)
    gathered = jnp.take(window, local_index, axis=2)
    opened = (neighbours >= 0).astype(jnp.float32)
    spread = spread_sum(tracers, pick_halos(gathered, row_count, col_count), opened)
    stepped = tracers + horizontal_diffusivity * spread + vertical
    buoyancy = 0.6 * stepped[0] + 0.05 * stepped[0] * stepped[0] - 0.8 * stepped[1]
    thickness = lax.dynamic_slice_in_dim(layer_thickness, first_level, levels_here)
    weighted = thickness[:, None, None, None] * buoyancy
    local_column = jnp.cumsum(weighted, axis=0)
    own_total = local_column[-1]
    prefix = prefix_2(
        own_total, "lev", lambda earlier, later: earlier + later, jnp.zeros_like(own_total)
    )
    column = prefix[None] + local_column
    neighbour_float = neighbours.astype(jnp.float32)
    summed = lax.psum(own_total, "lev")
    pooled_force, pooled_diag, pooled_lists = (
        lax.all_gather(summed, "sub", axis=0, tiled=True),
        lax.all_gather(surface_diagonal, "sub", axis=0, tiled=True),
        lax.all_gather(neighbour_float, "sub", axis=0, tiled=True),
    )
    list_place = baro_blocks - group_base
    occupied = baro_blocks >= 0
    safe_location = jnp.clip(list_place, 0, pooled_force.shape[0] - 1)
    safe_list = jnp.clip(list_place, 0, pooled_lists.shape[0] - 1)
    forcing_slots = jnp.where(
        occupied[:, None, None], jnp.take(pooled_force, safe_location, axis=0), 0.0
    )
    diagonal_slots = jnp.where(
        occupied[:, None, None], jnp.take(pooled_diag, safe_location, axis=0), 1.0
    )
    slot_lists = jnp.where(occupied[:, None], jnp.take(pooled_lists, safe_list, axis=0), -1.0)
    window_ranks = tropic_window((baro_blocks + 1).astype(jnp.float32))
    group_ranks = window_ranks[peer_count * slot_count : 2 * peer_count * slot_count]
    slot_index = find_places(window_ranks, (slot_lists + 1.0).reshape(-1)).reshape(slot_count, 4)
    slot_open = (slot_lists >= 0.0).astype(jnp.float32)

    def squares(values):
        return lax.psum(jnp.sum(values * values), ("blk", "sub", "lev"))

    solution = jnp.zeros_like(forcing_slots)
    residual = forcing_slots
    direction = forcing_slots
    norm_now = squares(residual)
    for iteration in range(ITERS):
        halo_source = jnp.take(tropic_window(edge_strips(direction)), slot_index, axis=0)
        applied = diagonal_slots * direction - spread_sum(
            direction, pick_halos(halo_source, row_count, col_count), slot_open
        )
        step_size = norm_now / lax.psum(jnp.sum(direction * applied), ("blk", "sub", "lev"))
        solution = solution + step_size * direction
        residual = residual - step_size * applied
        norm_next = squares(residual)
        direction = residual + norm_next / norm_now * direction
        norm_now = norm_next
    heights = lax.all_gather(solution, ("sub", "lev"), axis=0, tiled=True)
    targets = (
        group_base + sub_index * owned_blocks + jnp.arange(owned_blocks, dtype=jnp.int32) + 1
    ).astype(jnp.float32)
    eta_blocks = jnp.take(heights, find_places(group_ranks, targets), axis=0)
    pressure = eta_blocks[None] - column
    return (stepped, pressure, solution)


def solution(mesh):
    placed = (
        P("grp", "lev", ("blk", "sub"), None, None),
        P(("blk", "sub"), None, None),
        P(),
        P(),
        P(("blk", "sub"), None, None),
        P(("blk", "sub"), None),
        P(("blk", "sub", "lev")),
    )
    return jax.shard_map(
        local,
        mesh=mesh,
        in_specs=placed,
        out_specs=(
            P("grp", "lev", ("blk", "sub"), None, None),
            P(("grp", "lev"), ("blk", "sub"), None, None),
            P(("grp", "blk", "sub", "lev"), None, None),
        ),
        check_vma=False,
    )
```

profile of v0, /device:TPU:0, one launch (start us, length us, event | category | flops | bytes accessed | tf_op | source)
XLA Modules:
  0.0 310.5 jit_solution(7082916216071494237)
XLA Ops:
  4.7 6.9 %all_gather.30 = f32[2,10,8,288]{3,0,2,1:T(2,128)S(1)} all-gather(f32[2,10,4,288]{3,0,2,1:T(2,128)S(1)} %pad_maximum_fusion.1), channel_id=1, replica_groups=mesh['grp'=2,'blk'=4,'sub'=2,'lev'=2] {'sub'}, dimensions={2}, use_global_device_ids=true | all-gather | bytes 276480 | tf_op jit(solution)/shard_map/all_gather | solution.py:77
  11.6 4.4 %collective-permute-start = (f32[2,10,8,288]{3,0,2,1:T(2,128)S(1)}, f32[2,10,8,288]{3,0,2,1:T(2,128)}, u32[]{:S(2)}, u32[]{:S(2)}) collective-permute-start(f32[2,10,8,288]{3,0,2,1:T(2,128)S(1)} %all_gather.30), channel_id=1, source_target_pairs={{0,4},{4,8},{8,12},{1,5},{5,9},{9,13},{2,6},{6,10},{10,14},{3,7},{... | collective-permute-start | bytes 552968 | tf_op jit(solution)/shard_map/ppermute | solution.py:12
  20.0 6.2 %all-reduce = f32[12]{0:T(128)} all-reduce(f32[12]{0:T(128)S(1)} %convert_dynamic-update-slice_fusion), channel_id=1, replica_groups=mesh['grp'=2,'blk'=4,'sub'=2,'lev'=2] {'sub','lev'}, use_global_device_ids=true, to_apply=%add | all-reduce | flops 12 | bytes 96
  26.2 5.5 %collective-permute-start.6 = (f32[12]{0:T(128)}, f32[12]{0:T(128)}, u32[]{:S(2)}, u32[]{:S(2)}) collective-permute-start(f32[12]{0:T(128)} %all-reduce), channel_id=1, source_target_pairs={{0,4},{4,8},{8,12},{1,5},{5,9},{9,13},{2,6},{6,10},{10,14},{3,7},{... | collective-permute-start | bytes 152 | tf_op jit(solution)/shard_map/ppermute | solution.py:12
  39.3 4.3 %all-gather = f32[2,4,4]{2,1,0:T(4,128)S(1)} all-gather(f32[1,4,4]{2,1,0:T(4,128)S(1)} %convert_bitcast_fusion), channel_id=1, replica_groups=mesh['grp'=2,'blk'=4,'sub'=2,'lev'=2] {'sub'}, dimensions={0}, use_global_device_ids=true | all-gather | bytes 192 | tf_op jit(solution)/shard_map/all_gather | solution.py:149
  49.5 6.0 %all_gather.33 = f32[8,16,128]{2,1,0:T(8,128)} all-gather(f32[4,16,128]{2,1,0:T(8,128)} %param.15), channel_id=1, replica_groups=mesh['grp'=2,'blk'=4,'sub'=2,'lev'=2] {'sub'}, dimensions={0}, use_global_device_ids=true | all-gather | bytes 98304 | tf_op jit(solution)/shard_map/all_gather | solution.py:148
  62.9 2.7 collective-permute-start.3
  74.8 3.1 gather_fusion
  83.6 2.5 fusion.6
  87.1 3.4 %psum.49 = f32[4,16,128]{2,1,0:T(8,128)S(1)} all-reduce(f32[4,16,128]{2,1,0:T(8,128)S(1)} %get-tuple-element.63), channel_id=1, replica_groups=mesh['grp'=2,'blk'=4,'sub'=2,'lev'=2] {'lev'}, use_global_device_ids=true, to_apply=%region_2.3 | all-reduce | flops 8192 | bytes 65536 | tf_op jit(solution)/shard_map/psum | solution.py:145
  90.5 4.6 %all_gather.32 = f32[8,16,128]{2,1,0:T(8,128)S(1)} all-gather(f32[4,16,128]{2,1,0:T(8,128)S(1)} %psum.49), channel_id=1, replica_groups=mesh['grp'=2,'blk'=4,'sub'=2,'lev'=2] {'sub'}, dimensions={0}, use_global_device_ids=true | all-gather | bytes 98304 | tf_op jit(solution)/shard_map/all_gather | solution.py:147
  96.1 5.2 %all-gather.1 = f32[4,3,288]{2,1,0:T(4,128)S(1)} all-gather(f32[1,3,288]{2,1,0:T(4,128)S(1)} %maximum_bitcast_fusion), channel_id=1, replica_groups=mesh['grp'=2,'blk'=4,'sub'=2,'lev'=2] {'sub','lev'}, dimensions={0}, use_global_device_ids=true | all-gather | bytes 17280 | tf_op jit(solution)/shard_map/all_gather | solution.py:84
  101.3 4.5 %collective-permute-start.4 = (f32[12,288]{1,0:T(8,128)S(1)}, f32[12,288]{1,0:T(8,128)S(1)}, u32[]{:S(2)}, u32[]{:S(2)}) collective-permute-start(f32[12,288]{1,0:T(8,128)S(1)} %reshape.194), channel_id=1, source_target_pairs={{0,4},{4,8},{8,12},{1,5},{5,9},{9,13},{2,6},{6,10},{10,14},{3,7},{... | collective-permute-start | bytes 41480 | tf_op jit(solution)/shard_map/ppermute | solution.py:12
  107.3 4.2 %collective-permute-done.5 = f32[12,288]{1,0:T(8,128)S(1)} collective-permute-done((f32[12,288]{1,0:T(8,128)S(1)}, f32[12,288]{1,0:T(8,128)S(1)}, u32[]{:S(2)}, u32[]{:S(2)}) %collective-permute-start.5) | collective-permute-done | bytes 13856 | tf_op jit(solution)/shard_map/ppermute | solution.py:12
  114.5 30.1 %all-reduce.1 = (f32[]{:T(128)}, f32[]{:T(128)}) all-reduce(f32[]{:T(128)} %get-tuple-element.25, f32[]{:T(128)} %get-tuple-element.24), channel_id=1, replica_groups=mesh['grp'=2,'blk'=4,'sub'=2,'lev'=2] {'blk','sub','lev'}, use_global_device_ids=true, to_apply=%region_4.6 | all-reduce | flops 2 | bytes 16 | tf_op jit(solution)/shard_map/psum | solution.py:168
  146.6 30.1 %psum.52 = f32[]{:T(128)} all-reduce(f32[]{:T(128)} %get-tuple-element.40), channel_id=1, replica_groups=mesh['grp'=2,'blk'=4,'sub'=2,'lev'=2] {'blk','sub','lev'}, use_global_device_ids=true, to_apply=%region_9.12 | all-reduce | flops 1 | bytes 8 | tf_op jit(solution)/shard_map/psum | solution.py:168
  178.4 5.2 %all-gather.2 = f32[4,3,288]{2,1,0:T(4,128)S(1)} all-gather(f32[1,3,288]{2,1,0:T(4,128)S(1)} %maximum_bitcast_fusion.1), channel_id=1, replica_groups=mesh['grp'=2,'blk'=4,'sub'=2,'lev'=2] {'sub','lev'}, dimensions={0}, use_global_device_ids=true | all-gather | bytes 17280 | tf_op jit(solution)/shard_map/all_gather | solution.py:84
  186.4 4.2 %collective-permute-done.9 = f32[12,288]{1,0:T(8,128)S(1)} collective-permute-done((f32[12,288]{1,0:T(8,128)S(1)}, f32[12,288]{1,0:T(8,128)S(1)}, u32[]{:S(2)}, u32[]{:S(2)}) %collective-permute-start.9) | collective-permute-done | bytes 13856 | tf_op jit(solution)/shard_map/ppermute | solution.py:12
  192.3 30.1 %psum.53 = f32[]{:T(128)} all-reduce(f32[]{:T(128)} %get-tuple-element.38), channel_id=1, replica_groups=mesh['grp'=2,'blk'=4,'sub'=2,'lev'=2] {'blk','sub','lev'}, use_global_device_ids=true, to_apply=%region_11.14 | all-reduce | flops 1 | bytes 8 | tf_op jit(solution)/shard_map/psum | solution.py:179
  226.2 30.3 %psum.54 = f32[]{:T(128)} all-reduce(f32[]{:T(128)} %multiply_reduce_fusion), channel_id=1, replica_groups=mesh['grp'=2,'blk'=4,'sub'=2,'lev'=2] {'blk','sub','lev'}, use_global_device_ids=true, to_apply=%region_13.16 | all-reduce | flops 1 | bytes 8 | tf_op jit(solution)/shard_map/psum | solution.py:168
  258.0 5.2 %all-gather.3 = f32[4,3,288]{2,1,0:T(4,128)S(1)} all-gather(f32[1,3,288]{2,1,0:T(4,128)S(1)} %maximum_bitcast_fusion.2), channel_id=1, replica_groups=mesh['grp'=2,'blk'=4,'sub'=2,'lev'=2] {'sub','lev'}, dimensions={0}, use_global_device_ids=true | all-gather | bytes 17280 | tf_op jit(solution)/shard_map/all_gather | solution.py:84
  266.0 4.2 %collective-permute-done.11 = f32[12,288]{1,0:T(8,128)S(1)} collective-permute-done((f32[12,288]{1,0:T(8,128)S(1)}, f32[12,288]{1,0:T(8,128)S(1)}, u32[]{:S(2)}, u32[]{:S(2)}) %collective-permute-start.11) | collective-permute-done | bytes 13856 | tf_op jit(solution)/shard_map/ppermute | solution.py:12
  271.9 30.1 %psum.55 = f32[]{:T(128)} all-reduce(f32[]{:T(128)} %fusion.39), channel_id=1, replica_groups=mesh['grp'=2,'blk'=4,'sub'=2,'lev'=2] {'blk','sub','lev'}, use_global_device_ids=true, to_apply=%region_15.18 | all-reduce | flops 1 | bytes 8 | tf_op jit(solution)/shard_map/psum | solution.py:179
  303.5 5.3 %all_gather.38 = f32[12,16,128]{2,1,0:T(8,128)S(1)} all-gather(f32[3,16,128]{2,1,0:T(8,128)S(1)} %multiply_add_fusion), channel_id=1, replica_groups=mesh['grp'=2,'blk'=4,'sub'=2,'lev'=2] {'sub','lev'}, dimensions={0}, use_global_device_ids=true | all-gather | bytes 122880 | tf_op jit(solution)/shard_map/all_gather | solution.py:185
  (214 shorter events, 63.6 us)
Async XLA Ops:
  4.0 29.0 %copy-start = (f32[2,10,4,16,128]{4,3,2,1,0:T(8,128)S(1)}, f32[2,10,4,16,128]{4,3,2,1,0:T(8,128)}, u32[]{:S(2)}) copy-start(f32[2,10,4,16,128]{4,3,2,1,0:T(8,128)} %param.11) | copy-start | bytes 1966084
  11.6 60.9 %collective-permute-start = (f32[2,10,8,288]{3,0,2,1:T(2,128)S(1)}, f32[2,10,8,288]{3,0,2,1:T(2,128)}, u32[]{:S(2)}, u32[]{:S(2)}) collective-permute-start(f32[2,10,8,288]{3,0,2,1:T(2,128)S(1)} %all_gather.30), channel_id=1, source_target_pairs={{0,4},{4,8},{8,12},{1,5},{5,9},{9,13},{2,6},{6,10},{10,14},{3,7},{... | collective-permute-start | bytes 552968 | tf_op jit(solution)/shard_map/ppermute | solution.py:12
  18.7 53.9 %collective-permute-start.1 = (f32[2,10,8,288]{3,0,2,1:T(2,128)S(1)}, f32[2,10,8,288]{3,0,2,1:T(2,128)}, u32[]{:S(2)}, u32[]{:S(2)}) collective-permute-start(f32[2,10,8,288]{3,0,2,1:T(2,128)S(1)} %all_gather.30), channel_id=1, source_target_pairs={{4,0},{8,4},{12,8},{5,1},{9,5},{13,9},{6,2},{10,6},{14,10},{7,3},{... | collective-permute-start | bytes 552968 | tf_op jit(solution)/shard_map/ppermute | solution.py:12
  26.2 36.7 %collective-permute-start.6 = (f32[12]{0:T(128)}, f32[12]{0:T(128)}, u32[]{:S(2)}, u32[]{:S(2)}) collective-permute-start(f32[12]{0:T(128)} %all-reduce), channel_id=1, source_target_pairs={{0,4},{4,8},{8,12},{1,5},{5,9},{9,13},{2,6},{6,10},{10,14},{3,7},{... | collective-permute-start | bytes 152 | tf_op jit(solution)/shard_map/ppermute | solution.py:12
  31.6 34.0 %collective-permute-start.7 = (f32[12]{0:T(128)}, f32[12]{0:T(128)}, u32[]{:S(2)}, u32[]{:S(2)}) collective-permute-start(f32[12]{0:T(128)} %all-reduce), channel_id=1, source_target_pairs={{4,0},{8,4},{12,8},{5,1},{9,5},{13,9},{6,2},{10,6},{14,10},{7,3},{... | collective-permute-start | bytes 152 | tf_op jit(solution)/shard_map/ppermute | solution.py:12
  33.6 49.3 %collective-permute-start.2 = (f32[2,1,4,16,128]{4,3,2,1,0:T(8,128)}, f32[2,1,4,16,128]{4,3,2,1,0:T(8,128)}, u32[]{:S(2)}, u32[]{:S(2)}) collective-permute-start(f32[2,1,4,16,128]{4,3,2,1,0:T(8,128)} %get-tuple-element.48), channel_id=1, source_target_pairs={{1,0},{3,2},{5,4},{7,6},{9,8},{11,10},{13,12},{15,14},{17,16},{19,... | collective-permute-start | bytes 196616 | tf_op jit(solution)/shard_map/ppermute | solution.py:23
  38.8 4.8 %copy-start.24 = (s32[1024]{0:T(1024)}, s32[1024]{0:T(1024)S(1)}, u32[]{:S(2)}) copy-start(s32[1024]{0:T(1024)S(1)} %pad_clamp_fusion.2) | copy-start | bytes 12292
  62.9 3.4 %copy-start.35 = (f32[12]{0:T(128)S(1)}, f32[12]{0:T(128)}, u32[]{:S(2)}) copy-start(f32[12]{0:T(128)} %add.185) | copy-start | bytes 148
  62.9 20.0 %collective-permute-start.3 = (f32[2,1,4,16,128]{4,3,2,1,0:T(8,128)}, f32[2,1,4,16,128]{4,3,2,1,0:T(8,128)}, u32[]{:S(2)}, u32[]{:S(2)}) collective-permute-start(f32[2,1,4,16,128]{4,3,2,1,0:T(8,128)} %get-tuple-element.47), channel_id=1, source_target_pairs={{0,1},{2,3},{4,5},{6,7},{8,9},{10,11},{12,13},{14,15},{16,17},{18,... | collective-permute-start | bytes 196616 | tf_op jit(solution)/shard_map/ppermute | solution.py:20
  70.8 1.2 copy-start.9
  83.6 3.4 %copy-start.32 = (f32[10]{0:T(128)S(1)}, f32[10]{0:T(128)}, u32[]{:S(2)}) copy-start(f32[10]{0:T(128)} %dynamic_slice.15) | copy-start | bytes 124
  101.3 6.1 %collective-permute-start.4 = (f32[12,288]{1,0:T(8,128)S(1)}, f32[12,288]{1,0:T(8,128)S(1)}, u32[]{:S(2)}, u32[]{:S(2)}) collective-permute-start(f32[12,288]{1,0:T(8,128)S(1)} %reshape.194), channel_id=1, source_target_pairs={{0,4},{4,8},{8,12},{1,5},{5,9},{9,13},{2,6},{6,10},{10,14},{3,7},{... | collective-permute-start | bytes 41480 | tf_op jit(solution)/shard_map/ppermute | solution.py:12
  105.8 5.7 %collective-permute-start.5 = (f32[12,288]{1,0:T(8,128)S(1)}, f32[12,288]{1,0:T(8,128)S(1)}, u32[]{:S(2)}, u32[]{:S(2)}) collective-permute-start(f32[12,288]{1,0:T(8,128)S(1)} %reshape.194), channel_id=1, source_target_pairs={{4,0},{8,4},{12,8},{5,1},{9,5},{13,9},{6,2},{10,6},{14,10},{7,3},{... | collective-permute-start | bytes 41480 | tf_op jit(solution)/shard_map/ppermute | solution.py:12
  107.2 4.3 %copy-start.8 = (s32[1024]{0:T(1024)S(1)}, s32[1024]{0:T(1024)}, u32[]{:S(2)}) copy-start(s32[1024]{0:T(1024)} %pad_clamp_fusion.1) | copy-start | bytes 12292
  112.1 1.0 copy-start.17
  112.2 1.0 copy-start.18
  112.2 1.0 copy-start.19
  112.2 1.0 copy-start.20
  112.2 1.0 copy-start.21
  183.6 2.8 collective-permute-start.8
  184.9 5.7 %collective-permute-start.9 = (f32[12,288]{1,0:T(8,128)S(1)}, f32[12,288]{1,0:T(8,128)S(1)}, u32[]{:S(2)}, u32[]{:S(2)}) collective-permute-start(f32[12,288]{1,0:T(8,128)S(1)} %reshape.196), channel_id=1, source_target_pairs={{4,0},{8,4},{12,8},{5,1},{9,5},{13,9},{6,2},{10,6},{14,10},{7,3},{... | collective-permute-start | bytes 41480 | tf_op jit(solution)/shard_map/ppermute | solution.py:12
  263.2 2.8 collective-permute-start.10
  264.5 5.7 %collective-permute-start.11 = (f32[12,288]{1,0:T(8,128)S(1)}, f32[12,288]{1,0:T(8,128)S(1)}, u32[]{:S(2)}, u32[]{:S(2)}) collective-permute-start(f32[12,288]{1,0:T(8,128)S(1)} %reshape.198), channel_id=1, source_target_pairs={{4,0},{8,4},{12,8},{5,1},{9,5},{13,9},{6,2},{10,6},{14,10},{7,3},{... | collective-permute-start | bytes 41480 | tf_op jit(solution)/shard_map/ppermute | solution.py:12
  303.5 5.3 %copy-start.6 = (f32[3,16,128]{2,1,0:T(8,128)}, f32[3,16,128]{2,1,0:T(8,128)S(1)}, u32[]{:S(2)}) copy-start(f32[3,16,128]{2,1,0:T(8,128)S(1)} %multiply_add_fusion) | copy-start | bytes 73732
  (26 other events, 18.2 us)
where the time goes:
time: 312 us; the launch traced here: 310 us
  blocking collectives  205 us (66%)
  local copies, waits for them, and re-layouts  32.2 us (10%)
  starting transfers between devices  27.4 us (9%)
  other arithmetic  24.5 us (8%)
  waiting for transfers between devices  13 us (4%)
  between operations  8.55 us (3%)
    psum x3, blocking collectives, squares(): return lax.psum(jnp.sum(values * values), ('blk', 'sub', 'lev'))  90.5 us
    psum x2, blocking collectives, local(): lax.psum(jnp.sum(direction * applied), ('blk', 'sub', 'lev'))  60.2 us
    ppermute x10, starting transfers between devices, passed_along(): return lax.ppermute(block, axis, route)  23.5 us
    all_gather x3, blocking collectives, tropic_window(): together = lax.all_gather(values, ('sub', 'lev'), axis=0, tiled=True)  15.5 us
    ppermute x10, waiting for transfers between devices, passed_along(): return lax.ppermute(block, axis, route)  13 us
    unnamed x87, local copies, waits for them, and re-layouts  7.33 us
    all_gather x1, blocking collectives, clinic_window(): together = lax.all_gather(strips, 'sub', axis=2, tiled=True)  6.92 us
  transfers between devices with their start and end apart: 12, of which 6 were waited for; matrix products, arithmetic and copies ran while one was open for 11% of the time, Pallas kernels for 0%

commit v1 on v0

v1 whole, which is shorter than its diff:
```python
import functools

import jax
import jax.numpy as jnp
from jax import lax
from jax.experimental import pallas as pl
from jax.experimental.pallas import tpu as pltpu
from jax.sharding import PartitionSpec as P

ITERS = 3
F32 = jnp.float32
HIGH = lax.Precision.HIGHEST


def five_point(v, before, after, up, down, west, east, q, row, lane):
    rows, cols = v.shape
    xw = jnp.where(lane == cols - 1, jnp.where(west == q - 1, before, after), v)
    xe = jnp.where(lane == 0, jnp.where(east == q - 1, before, after), v)
    dw = jnp.where((lane == 0) & (west < 0), 0.0, pltpu.roll(xw, 1, 1) - v)
    de = jnp.where((lane == cols - 1) & (east < 0), 0.0, pltpu.roll(xe, cols - 1, 1) - v)
    fa = jnp.where(row == 0, jnp.broadcast_to(up, v.shape), pltpu.roll(v, 1, 0))
    fb = jnp.where(row == rows - 1, jnp.broadcast_to(down, v.shape), pltpu.roll(v, rows - 1, 0))
    return (fa - v) + (fb - v) + dw + de


def kernel(
    B, S, ITEMS,
    tr, hd, vm, lt, sd, nb, baro,
    out_tr, out_p, out_s,
    X, Y, C, TOPS, BOTS, HA, HB, CP, CR, TOT, TIN, M, NBI, G, E, D, AP, T, BT, PA, PB, QA, QB,
    loc, lev_sem, bot_s, bot_r, top_s, top_r, col_s, col_r, m_s, m_r, g_s, g_r, core_s, core_r,
):
    L, NBD, RC, CC = ITEMS
    BS = B * S
    NR = BS * NBD
    H = NBD // 2
    R8 = 2 * NBD
    blk, sub, lev = lax.axis_index("blk"), lax.axis_index("sub"), lax.axis_index("lev")
    me = blk * S + sub
    other = 1 - lev
    row = lax.broadcasted_iota(jnp.int32, (RC, CC), 0)
    lane = lax.broadcasted_iota(jnp.int32, (RC, CC), 1)

    def at_dev(d):
        return {"blk": d // S, "sub": d % S, "lev": lev}

    barrier = pltpu.get_barrier_semaphore()
    pl.semaphore_signal(barrier, inc=1, device_id={"lev": other}, device_id_type=pl.DeviceIdType.MESH)

    @pl.loop(1, BS)
    def _(d):
        pl.semaphore_signal(
            barrier, inc=1, device_id=at_dev((me + d) % BS), device_id_type=pl.DeviceIdType.MESH
        )

    load = pltpu.make_async_copy(tr, X.at[:, 1 : L + 1], loc.at[0])
    load.start()

    def remote(src, dst, ss, rs, dev):
        return pltpu.make_async_remote_copy(
            src_ref=src, dst_ref=dst, send_sem=ss, recv_sem=rs, device_id=dev,
            device_id_type=pl.DeviceIdType.MESH,
        )

    to_core = {"lev": other}
    MR = H * RC
    for j in range(H):
        M[me, lev, j * RC : (j + 1) * RC, :] = sd[lev * H + j]
    r8 = lax.broadcasted_iota(jnp.int32, (H * 4, CC), 0)
    lists = jnp.zeros((H * 4, CC), jnp.int32)
    for j in range(H):
        for s in range(4):
            lists = jnp.where(r8 == j * 4 + s, nb[lev * H + j, s], lists)
    M[me, lev, MR : MR + H * 4, :] = lists.astype(F32)

    zero_edge = jnp.zeros((S, R8, L * CC), F32)
    zero_block = jnp.zeros((RC, CC), F32)

    @pl.when(blk == 0)
    def _():
        BOTS[0:S] = zero_edge

    @pl.when(blk == B - 1)
    def _():
        TOPS[S : 2 * S] = zero_edge

    @pl.when(me == 0)
    def _():
        CR[0] = zero_block

    @pl.when(me == BS - 1)
    def _():
        CR[1] = zero_block

    outer = lev * (L + 1)
    for t in range(2):
        for b in range(NBD):
            X[t, outer, b] = zero_block

    load.wait()
    pl.semaphore_wait(barrier, BS)

    level_copy = remote(
        tr.at[:, pl.ds(other * (L - 1), 1)],
        X.at[:, pl.ds(lev * (L + 1), 1)],
        lev_sem.at[0], lev_sem.at[1], to_core,
    )
    level_copy.start()

    my_top = sub
    my_bot = S + sub

    def pack(k, packed):
        first, last = packed
        lanes = pl.ds(pl.multiple_of(k * CC, CC), CC)
        for t in range(2):
            for b in range(NBD):
                TOPS[my_top, t * NBD + b : t * NBD + b + 1, lanes] = X[t, k + 1, b, 0:1, :]
                BOTS[my_bot, t * NBD + b : t * NBD + b + 1, lanes] = X[t, k + 1, b, RC - 1 : RC, :]
            spot = t * L + k
            mine = lax.shift_right_logical(lane, 1) == spot
            first = jnp.where(mine, pltpu.roll(X[t, k + 1, 0], 2 * spot + 1, 1), first)
            last = jnp.where(mine, pltpu.roll(X[t, k + 1, NBD - 1], 2 * spot + 1, 1), last)
        return first, last

    first, last = lax.fori_loop(0, L, pack, (zero_block, zero_block))
    CP[0] = first
    CP[1] = last

    def top_slot(i):
        return TOPS.at[i]

    def bot_slot(i):
        return BOTS.at[i]

    def bot_to(i):
        return remote(
            bot_slot(S + sub), bot_slot(sub + (S if i < S else 0)), bot_s.at[i],
            bot_r.at[sub + (S if i < S else 0)],
            {"blk": blk + (0 if i < S else 1), "sub": i % S, "lev": lev},
        )

    def top_to(i):
        return remote(
            top_slot(sub), top_slot(sub + (0 if i < S else S)), top_s.at[i],
            top_r.at[sub + (0 if i < S else S)],
            {"blk": blk - (0 if i < S else 1), "sub": i % S, "lev": lev},
        )

    def each_edge(act):
        for i in range(S, 2 * S):
            pl.when(blk < B - 1)(lambda i=i: act(bot_to(i)))
            pl.when(blk > 0)(lambda i=i: act(top_to(i)))
        for i in range(S):
            pl.when(sub != i)(lambda i=i: act(bot_to(i)))
            pl.when(sub != i)(lambda i=i: act(top_to(i)))

    def col_down():
        return remote(CP.at[0], CR.at[1], col_s.at[0], col_r.at[1], at_dev(jnp.maximum(me - 1, 0)))

    def col_up():
        return remote(CP.at[1], CR.at[0], col_s.at[1], col_r.at[0], at_dev(jnp.minimum(me + 1, BS - 1)))

    each_edge(lambda c: c.start())
    pl.when(me > 0)(lambda: col_down().start())
    pl.when(me < BS - 1)(lambda: col_up().start())

    def m_to(d):
        dev = (me + d) % BS
        return remote(M.at[me, lev], M.at[me, lev], m_s.at[dev], m_r.at[me], at_dev(dev))

    def m_from(d):
        dev = (me + d) % BS
        return remote(M.at[dev, lev], M.at[dev, lev], m_s.at[dev], m_r.at[dev], at_dev(dev))

    @pl.loop(1, BS)
    def _(d):
        m_to(d).start()

    n8 = lax.broadcasted_iota(jnp.int32, (R8, 2 * S * R8), 0)
    c8 = lax.broadcasted_iota(jnp.int32, (R8, 2 * S * R8), 1)
    nba = jnp.zeros((R8, 2 * S * R8), jnp.int32)
    nbb = jnp.zeros((R8, 2 * S * R8), jnp.int32)
    for b in range(NBD):
        nba = jnp.where(n8 % NBD == b, nb[b, 0], nba)
        nbb = jnp.where(n8 % NBD == b, nb[b, 1], nbb)
    same_t = (n8 // NBD) == ((c8 // NBD) % 2)
    place = (c8 // R8) * NBD + c8 % NBD
    base = blk * S * NBD
    sel_a = jnp.where(same_t & (nba == place + base - S * NBD), 1.0, 0.0)
    sel_b = jnp.where(same_t & (nbb == place + base), 1.0, 0.0)

    for i in range(S):
        pl.when(blk > 0)(lambda i=i: remote(bot_slot(i), bot_slot(i), bot_s.at[i], bot_r.at[i], to_core).wait_recv())
        pl.when(sub != i)(
            lambda i=i: remote(bot_slot(S + i), bot_slot(S + i), bot_s.at[i], bot_r.at[S + i], to_core).wait_recv()
        )
        pl.when(sub != i)(lambda i=i: remote(top_slot(i), top_slot(i), top_s.at[i], top_r.at[i], to_core).wait_recv())
        pl.when(blk < B - 1)(
            lambda i=i: remote(top_slot(S + i), top_slot(S + i), top_s.at[i], top_r.at[S + i], to_core).wait_recv()
        )
    pl.when(me > 0)(lambda: remote(CR.at[0], CR.at[0], col_s.at[0], col_r.at[0], to_core).wait_recv())
    pl.when(me < BS - 1)(lambda: remote(CR.at[1], CR.at[1], col_s.at[1], col_r.at[1], to_core).wait_recv())
    level_copy.wait_recv()

    picked_a = jnp.dot(sel_a, BOTS[...].reshape(2 * S * R8, L * CC), precision=HIGH, preferred_element_type=F32)
    picked_b = jnp.dot(sel_b, TOPS[...].reshape(2 * S * R8, L * CC), precision=HIGH, preferred_element_type=F32)
    w8 = lax.broadcasted_iota(jnp.int32, (R8, L * CC), 0)
    open_a = jnp.zeros((R8, L * CC), jnp.int32)
    open_b = jnp.zeros((R8, L * CC), jnp.int32)
    for b in range(NBD):
        open_a = jnp.where(w8 % NBD == b, nb[b, 0], open_a)
        open_b = jnp.where(w8 % NBD == b, nb[b, 1], open_b)
    HA[...] = jnp.where(open_a < 0, TOPS[my_top], picked_a)
    HB[...] = jnp.where(open_b < 0, BOTS[my_bot], picked_b)

    wests = [jnp.full((RC, CC), nb[b, 2], jnp.int32) for b in range(NBD)]
    easts = [jnp.full((RC, CC), nb[b, 3], jnp.int32) for b in range(NBD)]
    levels = lt.shape[0]

    def step(k, cols):
        lanes = pl.ds(pl.multiple_of(k * CC, CC), CC)
        g = lev * L + k
        above = jnp.where(g == 0, 0.0, vm[jnp.maximum(g - 1, 0)])
        below = jnp.where(g == levels - 1, 0.0, vm[jnp.minimum(g, levels - 2)])
        thick = lt[g]
        new = []
        ends = []
        for t in range(2):
            shift = CC - 1 - 2 * (t * L + k)
            ends.append((pltpu.roll(CR[0], shift, 1), pltpu.roll(CR[1], shift, 1)))
        for b in range(NBD):
            q = me * NBD + b
            nxt = []
            for t in range(2):
                v = X[t, k + 1, b]
                before = ends[t][0] if b == 0 else X[t, k + 1, b - 1]
                after = ends[t][1] if b == NBD - 1 else X[t, k + 1, b + 1]
                spread = five_point(
                    v, before, after, HA[t * NBD + b : t * NBD + b + 1, lanes],
                    HB[t * NBD + b : t * NBD + b + 1, lanes], wests[b], easts[b], q, row, lane,
                )
                vertical = below * (X[t, k + 2, b] - v) - above * (v - X[t, k, b])
                y = v + hd[b] * spread + vertical
                Y[t, k, b] = y
                nxt.append(y)
            weighted = thick * (0.6 * nxt[0] + 0.05 * nxt[0] * nxt[0] - 0.8 * nxt[1])
            col = cols[b] + weighted
            C[k, b] = col
            new.append(col)
        return tuple(new)

    totals = lax.fori_loop(0, L, step, (zero_block,) * NBD)
    for b in range(NBD):
        TOT[b] = totals[b]
    tot_copy = remote(TOT, TIN, core_s.at[0], core_r.at[0], to_core)
    tot_copy.start()
    store = pltpu.make_async_copy(Y, out_tr, loc.at[1])
    store.start()

    @pl.loop(1, BS)
    def _(d):
        m_from(d).wait_recv()

    m_core = remote(M.at[:, lev], M.at[:, lev], core_s.at[1], core_r.at[1], to_core)
    m_core.start()

    tot_copy.wait_recv()
    for j in range(H):
        G[me, lev, j] = TOT[lev * H + j] + TIN[lev * H + j]

    def g_to(d):
        dev = (me + d) % BS
        return remote(G.at[me, lev], G.at[me, lev], g_s.at[dev], g_r.at[me], at_dev(dev))

    def g_from(d):
        dev = (me + d) % BS
        return remote(G.at[dev, lev], G.at[dev, lev], g_s.at[dev], g_r.at[dev], at_dev(dev))

    @pl.loop(1, BS)
    def _(d):
        g_to(d).start()

    remote(M.at[:, other], M.at[:, other], core_s.at[1], core_r.at[1], to_core).wait_recv()

    @pl.loop(0, BS)
    def _(d):
        for l in range(2):
            NBI[pl.ds(pl.multiple_of(d * NBD * 4 + l * H * 4, 8), H * 4), :] = M[
                d, l, MR : MR + H * 4, :
            ].astype(jnp.int32)

    KP = T.shape[0]
    PA[...] = NBI[pl.ds(0, NR, stride=4), :]
    PB[...] = NBI[pl.ds(1, NR, stride=4), :]
    wide = lax.broadcasted_iota(jnp.int32, (NR, CC), 1)
    for c in range(KP // CC):
        QA[:, c * CC : (c + 1) * CC] = jnp.where(PA[...] == wide + c * CC, 1.0, 0.0)
        QB[:, c * CC : (c + 1) * CC] = jnp.where(PB[...] == wide + c * CC, 1.0, 0.0)
    if KP > NR:
        T[NR:KP, :] = jnp.zeros((KP - NR, CC), F32)
        BT[NR:KP, :] = jnp.zeros((KP - NR, CC), F32)
    D[0] = zero_block
    D[NR + 1] = zero_block

    @pl.loop(1, BS)
    def _(d):
        g_from(d).wait_recv()

    g_core = remote(G.at[:, lev], G.at[:, lev], core_s.at[2], core_r.at[2], to_core)
    g_core.start()
    remote(G.at[:, other], G.at[:, other], core_s.at[2], core_r.at[2], to_core).wait_recv()
    g_core.wait_send()

    @pl.loop(1, BS)
    def _(d):
        g_to(d).wait_send()

    def total(acc):
        return jnp.sum(jnp.sum(acc, axis=0, keepdims=True), axis=1, keepdims=True)

    def over_blocks(body, carry):
        def devs(d, carry):
            for b in range(NBD):
                carry = body(d, b, d * NBD + b, carry)
            return carry

        return lax.fori_loop(0, BS, devs, carry)

    def set_direction(q, d):
        D[q + 1] = d
        T[pl.ds(q, 1), :] = d[0:1, :]
        BT[pl.ds(q, 1), :] = d[RC - 1 : RC, :]

    def begin(d, b, q, acc):
        f = G[d, b // H, b % H]
        set_direction(q, f)
        E[q] = zero_block
        return acc + f * f

    norm_now = total(over_blocks(begin, zero_block))
    for iteration in range(ITERS):
        tops, bots = T[...], BT[...]
        up_rows = jnp.dot(QA[...], bots, precision=HIGH, preferred_element_type=F32)
        down_rows = jnp.dot(QB[...], tops, precision=HIGH, preferred_element_type=F32)
        HA2 = jnp.where(PA[...] < 0, T[0:NR, :], up_rows)
        HB2 = jnp.where(PB[...] < 0, BT[0:NR, :], down_rows)
        AP[NR] = zero_block
        T[0:NR, :] = HA2
        BT[0:NR, :] = HB2

        def apply(d, b, q, acc):
            v = D[q + 1]
            west = jnp.broadcast_to(NBI[pl.ds(q * 4 + 2, 1), :], (RC, CC))
            east = jnp.broadcast_to(NBI[pl.ds(q * 4 + 3, 1), :], (RC, CC))
            spread = five_point(
                v, D[q], D[q + 2], T[pl.ds(q, 1), :], BT[pl.ds(q, 1), :], west, east, q, row, lane
            )
            diag = M[d, b // H, (b % H) * RC : (b % H + 1) * RC, :]
            applied = diag * v - spread
            AP[q] = applied
            return acc + v * applied

        size = norm_now / total(over_blocks(apply, zero_block))

        def update(d, b, q, acc):
            E[q] = E[q] + size * D[q + 1]
            r = G[d, b // H, b % H] - size * AP[q]
            G[d, b // H, b % H] = r
            return acc + r * r

        if iteration == ITERS - 1:
            def finish(d, b, q, acc):
                E[q] = E[q] + size * D[q + 1]
                return acc

            over_blocks(finish, jnp.int32(0))
            break
        norm_next = total(over_blocks(update, zero_block))
        beta = norm_next / norm_now

        def turn(d, b, q, acc):
            set_direction(q, G[d, b // H, b % H] + beta * D[q + 1])
            return acc

        over_blocks(turn, jnp.int32(0))
        norm_now = norm_next

    levf = lev.astype(F32)
    eta = [E[me * NBD + b] - levf * TIN[b] for b in range(NBD)]

    def press(k, _):
        for b in range(NBD):
            C[k, b] = eta[b] - C[k, b]
        return 0

    lax.fori_loop(0, L, press, 0)
    p_store = pltpu.make_async_copy(C, out_p, loc.at[2])
    p_store.start()
    for s in range(baro.shape[0]):
        held = baro[s]
        out_s[s] = jnp.where(jnp.full((RC, CC), held, jnp.int32) >= 0, E[jnp.maximum(held, 0)], 0.0)

    level_copy.wait_send()
    each_edge(lambda c: c.wait_send())
    pl.when(me > 0)(lambda: col_down().wait_send())
    pl.when(me < BS - 1)(lambda: col_up().wait_send())

    @pl.loop(1, BS)
    def _(d):
        m_to(d).wait_send()

    tot_copy.wait_send()
    m_core.wait_send()
    store.wait()
    p_store.wait()


def local(tracers, horizontal_diffusivity, vertical_mixing, layer_thickness, surface_diagonal, neighbours, baro_blocks):
    B, S = lax.axis_size("blk"), lax.axis_size("sub")
    L, NBD, RC, CC = tracers.shape[1:]
    BS = B * S
    NR = BS * NBD
    H = NBD // 2
    R8 = 2 * NBD
    KP = -(-NR // CC) * CC
    vm = pltpu.VMEM
    dma = pltpu.SemaphoreType.DMA
    slots = baro_blocks.shape[0]
    scratch = [
        vm((2, L + 2, NBD, RC, CC), F32),
        vm((2, L, NBD, RC, CC), F32),
        vm((L, NBD, RC, CC), F32),
        vm((2 * S, R8, L * CC), F32),
        vm((2 * S, R8, L * CC), F32),
        vm((R8, L * CC), F32),
        vm((R8, L * CC), F32),
        vm((2, RC, CC), F32),
        vm((2, RC, CC), F32),
        vm((NBD, RC, CC), F32),
        vm((NBD, RC, CC), F32),
        vm((BS, 2, H * RC + H * 4, CC), F32),
        vm((NR * 4, CC), jnp.int32),
        vm((BS, 2, H, RC, CC), F32),
        vm((NR, RC, CC), F32),
        vm((NR + 2, RC, CC), F32),
        vm((NR + 1, RC, CC), F32),
        vm((KP, CC), F32),
        vm((KP, CC), F32),
        vm((NR, CC), jnp.int32),
        vm((NR, CC), jnp.int32),
        vm((NR, KP), F32),
        vm((NR, KP), F32),
        dma((3,)), dma((2,)), dma((2 * S,)), dma((2 * S,)), dma((2 * S,)), dma((2 * S,)),
        dma((2,)), dma((2,)), dma((BS,)), dma((BS,)), dma((BS,)), dma((BS,)), dma((3,)), dma((3,)),
    ]
    need = (10 * L * NBD + 7 * NR) * RC * CC * 4 + 4 * NR * KP * 4 + (8 << 20)
    smem = pl.BlockSpec(memory_space=pltpu.SMEM)
    vmem = pl.BlockSpec(memory_space=pltpu.VMEM)
    hbm = pl.BlockSpec(memory_space=pl.ANY)
    return pl.pallas_call(
        functools.partial(kernel, B, S, (L, NBD, RC, CC)),
        out_shape=(
            jax.ShapeDtypeStruct(tracers.shape, F32),
            jax.ShapeDtypeStruct((L, NBD, RC, CC), F32),
            jax.ShapeDtypeStruct((slots, RC, CC), F32),
        ),
        in_specs=[hbm, vmem, smem, smem, vmem, smem, smem],
        out_specs=(hbm, hbm, vmem),
        scratch_shapes=scratch,
        compiler_params=pltpu.CompilerParams(
            collective_id=0, has_side_effects=True, vmem_limit_bytes=need
        ),
    )(tracers, horizontal_diffusivity, vertical_mixing, layer_thickness, surface_diagonal, neighbours, baro_blocks)


def solution(mesh):
    placed = (
        P("grp", "lev", ("blk", "sub"), None, None),
        P(("blk", "sub"), None, None),
        P(),
        P(),
        P(("blk", "sub"), None, None),
        P(("blk", "sub"), None),
        P(("blk", "sub", "lev")),
    )
    return jax.shard_map(
        local,
        mesh=mesh,
        in_specs=placed,
        out_specs=(
            P("grp", "lev", ("blk", "sub"), None, None),
            P(("grp", "lev"), ("blk", "sub"), None, None),
            P(("grp", "blk", "sub", "lev"), None, None),
        ),
        check_vma=False,
    )
```

time: 312 us -> 33.9 us (0.11)
  blocking collectives: 205 us -> 0 us
  starting transfers between devices: 27.4 us -> 0 us
  Pallas kernels: 0 us -> 25.4 us
  local copies, waits for them, and re-layouts: 32.2 us -> 7.41 us
  other arithmetic: 24.5 us -> 0 us
  waiting for transfers between devices: 13 us -> 0 us
  between operations: 8.55 us -> 0.66 us
    psum x6 -> x0, blocking collectives: 154 us -> none  [the longest x3 90.5 us: squares(): return lax.psum(jnp.sum(values * values), ('blk', 'sub', 'lev'))]
    all_gather x9 -> x0, blocking collectives: 44.5 us -> none  [the longest x3 15.5 us: tropic_window(): together = lax.all_gather(values, ('sub', 'lev'), axis=0, tiled=True)]
    ppermute x12 -> x0, starting transfers between devices: 27.4 us -> none  [the longest x10 23.5 us: passed_along(): return lax.ppermute(block, axis, route)]
    pallas_call x0 -> x1, Pallas kernels: none -> 25.4 us  [local(): pl.pallas_call(functools.partial(kernel, B, S, (L, NBD, RC, CC)), out_sha...]
    ppermute x12 -> x0, waiting for transfers between devices: 13 us -> none  [the longest x10 13 us: passed_along(): return lax.ppermute(block, axis, route)]
    gather x11 -> x0, local copies, waits for them, and re-layouts: 8.37 us -> none  [the longest x1 3.08 us: local(): gathered = jnp.take(window, local_index, axis=2)]
    slice x26 -> x0, local copies, waits for them, and re-layouts: 7.31 us -> none  [the longest x4 2.03 us: edge_strips(): values[..., :, 0]]
    unnamed x1 -> x0, blocking collectives: 6.17 us -> none
  transfers between devices with their start and end apart: 12 -> 0, of which waited for: 6 -> 0; matrix products, arithmetic and copies ran while one was open for 11% -> 0% of each run, Pallas kernels for 0% -> 0%
where the time goes in v1:
time: 33.9 us; the launch traced here: 33.5 us
  Pallas kernels  25.4 us (75%)
  local copies, waits for them, and re-layouts  7.41 us (22%)
  between operations  0.66 us (2%)
    pallas_call x1, Pallas kernels, local(): pl.pallas_call(functools.partial(kernel, B, S, (L, NBD, RC, CC)), out_sha...  25.4 us
    unnamed x17, local copies, waits for them, and re-layouts  7.41 us

profile of v1, /device:TPU:0, one launch (start us, length us, event | category | flops | bytes accessed | tf_op | source)
XLA Modules:
  0.0 33.5 jit_solution(1860193567452259457)
XLA Ops:
  0.6 0.0 copy-start
  0.6 1.1 %copy-done = f32[2,10,4,16,128]{4,3,2,1,0:T(8,128)S(1)} copy-done((f32[2,10,4,16,128]{4,3,2,1,0:T(8,128)S(1)}, f32[2,10,4,16,128]{4,3,2,1,0:T(8,128)}, u32[]{:S(2)}) %copy-start) | copy-done | bytes 655384
  1.7 0.0 copy-start.1
  1.7 0.8 %copy-done.1 = f32[4,16,128]{2,1,0:T(8,128)S(1)} copy-done((f32[4,16,128]{2,1,0:T(8,128)S(1)}, f32[4,16,128]{2,1,0:T(8,128)}, u32[]{:S(2)}) %copy-start.1) | copy-done | bytes 32792
  2.5 0.0 copy-start.2
  2.5 0.8 %copy-done.2 = f32[4,16,128]{2,1,0:T(8,128)S(1)} copy-done((f32[4,16,128]{2,1,0:T(8,128)S(1)}, f32[4,16,128]{2,1,0:T(8,128)}, u32[]{:S(2)}) %copy-start.2) | copy-done | bytes 32792
  3.2 0.0 copy-start.3
  3.2 0.7 %copy-done.3 = s32[4,4]{1,0:T(4,128)S(1)} copy-done((s32[4,4]{1,0:T(4,128)S(1)}, s32[4,4]{1,0:T(4,128)}, u32[]{:S(2)}) %copy-start.3) | copy-done | bytes 88
  3.9 0.0 copy-start.4
  3.9 0.7 %copy-done.4 = f32[19]{0:T(128)S(1)} copy-done((f32[19]{0:T(128)S(1)}, f32[19]{0:T(128)}, u32[]{:S(2)}) %copy-start.4) | copy-done | bytes 100
  4.6 0.0 copy-start.5
  4.6 0.7 %copy-done.5 = f32[20]{0:T(128)S(1)} copy-done((f32[20]{0:T(128)S(1)}, f32[20]{0:T(128)}, u32[]{:S(2)}) %copy-start.5) | copy-done | bytes 104
  5.2 0.0 copy-start.6
  5.2 0.7 %copy-done.6 = s32[3]{0:T(128)S(1)} copy-done((s32[3]{0:T(128)S(1)}, s32[3]{0:T(128)}, u32[]{:S(2)}) %copy-start.6) | copy-done | bytes 36
  5.9 25.4 %shard_map.94 = (f32[2,10,4,16,128]{4,3,2,1,0:T(8,128)S(1)}, f32[10,4,16,128]{3,2,1,0:T(8,128)S(1)}, f32[3,16,128]{2,1,0:T(8,128)S(1)}) custom-call(f32[2,10,4,16,128]{4,3,2,1,0:T(8,128)S(1)} %copy-done, f32[4,16,128]{2,1,0:T(8,128)S(1)} %copy-done.1, f32[19]{0:T(128)S(1)} %copy-done.4, f32[20]{0:T(128)S(1)} %copy-done.5, f32[4,16,128]{2,1,0:T(8,128)S(1)} %copy-done.2, ...), custom_call_target="tpu_custom_call" | custom-call | tf_op jit(solution)/shard_map/pallas_call | solution.py:461
  31.3 0.8 %copy.13 = f32[2,10,4,16,128]{4,3,2,1,0:T(8,128)} copy(f32[2,10,4,16,128]{4,3,2,1,0:T(8,128)S(1)} %get-tuple-element.6) | data formatting | bytes 1310720
  32.2 0.7 %copy.14 = f32[10,4,16,128]{3,2,1,0:T(8,128)} copy(f32[10,4,16,128]{3,2,1,0:T(8,128)S(1)} %get-tuple-element.7) | data formatting | bytes 655360
  32.9 0.6 %copy.15 = f32[3,16,128]{2,1,0:T(8,128)} copy(f32[3,16,128]{2,1,0:T(8,128)S(1)} %get-tuple-element.8) | data formatting | bytes 49152
Async XLA Ops:
  0.6 1.1 %copy-start = (f32[2,10,4,16,128]{4,3,2,1,0:T(8,128)S(1)}, f32[2,10,4,16,128]{4,3,2,1,0:T(8,128)}, u32[]{:S(2)}) copy-start(f32[2,10,4,16,128]{4,3,2,1,0:T(8,128)} %tr.1) | copy-start | bytes 1966084
  1.7 0.8 %copy-start.1 = (f32[4,16,128]{2,1,0:T(8,128)S(1)}, f32[4,16,128]{2,1,0:T(8,128)}, u32[]{:S(2)}) copy-start(f32[4,16,128]{2,1,0:T(8,128)} %hd.1) | copy-start | bytes 98308
  2.5 0.8 %copy-start.2 = (f32[4,16,128]{2,1,0:T(8,128)S(1)}, f32[4,16,128]{2,1,0:T(8,128)}, u32[]{:S(2)}) copy-start(f32[4,16,128]{2,1,0:T(8,128)} %sd.1) | copy-start | bytes 98308
  3.2 0.7 %copy-start.3 = (s32[4,4]{1,0:T(4,128)S(1)}, s32[4,4]{1,0:T(4,128)}, u32[]{:S(2)}) copy-start(s32[4,4]{1,0:T(4,128)} %nb.1) | copy-start | bytes 196
  3.9 0.7 %copy-start.4 = (f32[19]{0:T(128)S(1)}, f32[19]{0:T(128)}, u32[]{:S(2)}) copy-start(f32[19]{0:T(128)} %vm.1) | copy-start | bytes 232
  4.6 0.7 %copy-start.5 = (f32[20]{0:T(128)S(1)}, f32[20]{0:T(128)}, u32[]{:S(2)}) copy-start(f32[20]{0:T(128)} %lt.1) | copy-start | bytes 244
  5.2 0.7 %copy-start.6 = (s32[3]{0:T(128)S(1)}, s32[3]{0:T(128)}, u32[]{:S(2)}) copy-start(s32[3]{0:T(128)} %baro.1) | copy-start | bytes 40

commit v2 on v1

--- a/solution.py
+++ b/solution.py
@@ -25,9 +25,9 @@
 
 def kernel(
     B, S, ITEMS,
-    tr, hd, vm, lt, sd, nb, baro,
-    out_tr, out_p, out_s,
-    X, Y, C, TOPS, BOTS, HA, HB, CP, CR, TOT, TIN, M, NBI, G, E, D, AP, T, BT, PA, PB, QA, QB,
+    tr, hd_in, vm_in, lt_in, sd_in, nb_in, baro_in,
+    Y, C, out_s,
+    hd, vm, lt, sd, nb, baro, X, TOPS, BOTS, HA, HB, CP, CR, TOT, TIN, M, NBI, G, E, D, AP, T, BT, PA, PB, QA, QB,
     loc, lev_sem, bot_s, bot_r, top_s, top_r, col_s, col_r, m_s, m_r, g_s, g_r, core_s, core_r,
 ):
     L, NBD, RC, CC = ITEMS
@@ -44,6 +44,17 @@
     def at_dev(d):
         return {"blk": d // S, "sub": d % S, "lev": lev}
 
+    load = pltpu.make_async_copy(tr, X.at[:, 1 : L + 1], loc.at[0])
+    load.start()
+    small = [
+        pltpu.make_async_copy(source, target, loc.at[1 + i])
+        for i, (source, target) in enumerate(
+            [(nb_in, nb), (sd_in, sd), (hd_in, hd), (vm_in, vm), (lt_in, lt), (baro_in, baro)]
+        )
+    ]
+    for copy in small:
+        copy.start()
+
     barrier = pltpu.get_barrier_semaphore()
     pl.semaphore_signal(barrier, inc=1, device_id={"lev": other}, device_id_type=pl.DeviceIdType.MESH)
 
@@ -53,8 +64,6 @@
             barrier, inc=1, device_id=at_dev((me + d) % BS), device_id_type=pl.DeviceIdType.MESH
         )
 
-    load = pltpu.make_async_copy(tr, X.at[:, 1 : L + 1], loc.at[0])
-    load.start()
 
     def remote(src, dst, ss, rs, dev):
         return pltpu.make_async_remote_copy(
@@ -63,6 +72,8 @@
         )
 
     to_core = {"lev": other}
+    for copy in small:
+        copy.wait()
     MR = H * RC
     for j in range(H):
         M[me, lev, j * RC : (j + 1) * RC, :] = sd[lev * H + j]
@@ -255,8 +266,6 @@
         TOT[b] = totals[b]
     tot_copy = remote(TOT, TIN, core_s.at[0], core_r.at[0], to_core)
     tot_copy.start()
-    store = pltpu.make_async_copy(Y, out_tr, loc.at[1])
-    store.start()
 
     @pl.loop(1, BS)
     def _(d):
@@ -395,8 +404,6 @@
         return 0
 
     lax.fori_loop(0, L, press, 0)
-    p_store = pltpu.make_async_copy(C, out_p, loc.at[2])
-    p_store.start()
     for s in range(baro.shape[0]):
         held = baro[s]
         out_s[s] = jnp.where(jnp.full((RC, CC), held, jnp.int32) >= 0, E[jnp.maximum(held, 0)], 0.0)
@@ -412,8 +419,6 @@
 
     tot_copy.wait_send()
     m_core.wait_send()
-    store.wait()
-    p_store.wait()
 
 
 def local(tracers, horizontal_diffusivity, vertical_mixing, layer_thickness, surface_diagonal, neighbours, baro_blocks):
@@ -427,10 +432,15 @@
     vm = pltpu.VMEM
     dma = pltpu.SemaphoreType.DMA
     slots = baro_blocks.shape[0]
+    smem = pltpu.SMEM
     scratch = [
+        vm((NBD, RC, CC), F32),
+        smem(vertical_mixing.shape, F32),
+        smem(layer_thickness.shape, F32),
+        vm((NBD, RC, CC), F32),
+        smem(neighbours.shape, jnp.int32),
+        smem(baro_blocks.shape, jnp.int32),
         vm((2, L + 2, NBD, RC, CC), F32),
-        vm((2, L, NBD, RC, CC), F32),
-        vm((L, NBD, RC, CC), F32),
         vm((2 * S, R8, L * CC), F32),
         vm((2 * S, R8, L * CC), F32),
         vm((R8, L * CC), F32),
@@ -451,27 +461,54 @@
         vm((NR, CC), jnp.int32),
         vm((NR, KP), F32),
         vm((NR, KP), F32),
-        dma((3,)), dma((2,)), dma((2 * S,)), dma((2 * S,)), dma((2 * S,)), dma((2 * S,)),
+        dma((7,)), dma((2,)), dma((2 * S,)), dma((2 * S,)), dma((2 * S,)), dma((2 * S,)),
         dma((2,)), dma((2,)), dma((BS,)), dma((BS,)), dma((BS,)), dma((BS,)), dma((3,)), dma((3,)),
     ]
     need = (10 * L * NBD + 7 * NR) * RC * CC * 4 + 4 * NR * KP * 4 + (8 << 20)
-    smem = pl.BlockSpec(memory_space=pltpu.SMEM)
     vmem = pl.BlockSpec(memory_space=pltpu.VMEM)
-    hbm = pl.BlockSpec(memory_space=pl.ANY)
-    return pl.pallas_call(
+    hbm = pl.BlockSpec(memory_space=pltpu.HBM)
+    shapes = (
+        jax.ShapeDtypeStruct(tracers.shape, F32),
+        jax.ShapeDtypeStruct((L, NBD, RC, CC), F32),
+        jax.ShapeDtypeStruct((slots, RC, CC), F32),
+    )
+    results = pl.pallas_call(
         functools.partial(kernel, B, S, (L, NBD, RC, CC)),
-        out_shape=(
-            jax.ShapeDtypeStruct(tracers.shape, F32),
-            jax.ShapeDtypeStruct((L, NBD, RC, CC), F32),
-            jax.ShapeDtypeStruct((slots, RC, CC), F32),
-        ),
-        in_specs=[hbm, vmem, smem, smem, vmem, smem, smem],
-        out_specs=(hbm, hbm, vmem),
+        out_shape=shapes,
+        in_specs=[hbm] * 7,
+        out_specs=(vmem,) * 3,
         scratch_shapes=scratch,
         compiler_params=pltpu.CompilerParams(
             collective_id=0, has_side_effects=True, vmem_limit_bytes=need
         ),
-    )(tracers, horizontal_diffusivity, vertical_mixing, layer_thickness, surface_diagonal, neighbours, baro_blocks)
+    )(*[
+        pltpu.with_memory_space_constraint(x, pltpu.HBM)
+        for x in (
+            tracers, horizontal_diffusivity, vertical_mixing, layer_thickness, surface_diagonal,
+            neighbours, baro_blocks,
+        )
+    ])
+    return pl.pallas_call(
+        write_out,
+        out_shape=shapes,
+        in_specs=[vmem] * 3,
+        out_specs=(hbm,) * 3,
+        scratch_shapes=[dma((4,))],
+        compiler_params=pltpu.CompilerParams(vmem_limit_bytes=8 << 20),
+    )(*results)
+
+
+def write_out(tr, p, s, out_tr, out_p, out_s, sem):
+    copies = [
+        pltpu.make_async_copy(tr.at[0], out_tr.at[0], sem.at[0]),
+        pltpu.make_async_copy(tr.at[1], out_tr.at[1], sem.at[1]),
+        pltpu.make_async_copy(p, out_p, sem.at[2]),
+        pltpu.make_async_copy(s, out_s, sem.at[3]),
+    ]
+    for copy in copies:
+        copy.start()
+    for copy in copies:
+        copy.wait()
 
 
 def solution(mesh):

time: 33.9 us -> 26.5 us (0.78)
  local copies, waits for them, and re-layouts: 7.41 us -> 0 us
    unnamed x17 -> x0, local copies, waits for them, and re-layouts: 7.41 us -> none
    pallas_call x0 -> x1, Pallas kernels: none -> 0.98 us  [local(): pl.pallas_call(write_out, out_shape=shapes, in_specs=[vmem] * 3, out_spec...]
    pallas_call x1, Pallas kernels: 25.4 us -> 24.8 us  [local(): pl.pallas_call(functools.partial(kernel, B, S, (L, NBD, RC, CC)), out_sha...]
where the time goes in v2:
time: 26.5 us; the launch traced here: 26.4 us
  Pallas kernels  25.7 us (97%)
  between operations  0.64 us (2%)
    pallas_call x1, Pallas kernels, local(): pl.pallas_call(functools.partial(kernel, B, S, (L, NBD, RC, CC)), out_sha...  24.8 us
    pallas_call x1, Pallas kernels, local(): pl.pallas_call(write_out, out_shape=shapes, in_specs=[vmem] * 3, out_spec...  0.98 us

profile of v2, /device:TPU:0, one launch (start us, length us, event | category | flops | bytes accessed | tf_op | source)
XLA Modules:
  0.0 26.4 jit_solution(16826992082218831899)
XLA Ops:
  0.6 24.8 %shard_map.94 = (f32[2,10,4,16,128]{4,3,2,1,0:T(8,128)S(1)}, f32[10,4,16,128]{3,2,1,0:T(8,128)S(1)}, f32[3,16,128]{2,1,0:T(8,128)S(1)}) custom-call(f32[2,10,4,16,128]{4,3,2,1,0:T(8,128)} %tr.1, f32[4,16,128]{2,1,0:T(8,128)} %hd_in.1, f32[19]{0:T(128)} %vm_in.1, f32[20]{0:T(128)} %lt_in.1, f32[4,16,128]{2,1,0:T(8,128)} %sd_in.1, s32[4,4]{1,0:T(4,128)} %nb_in.1, ...), custom_call_target="tpu_custom_call" | custom-call | tf_op jit(solution)/shard_map/pallas_call | solution.py:475
  25.4 1.0 %shard_map.95 = (f32[2,10,4,16,128]{4,3,2,1,0:T(8,128)}, f32[10,4,16,128]{3,2,1,0:T(8,128)}, f32[3,16,128]{2,1,0:T(8,128)}) custom-call(f32[2,10,4,16,128]{4,3,2,1,0:T(8,128)S(1)} %get-tuple-element.6.tr, f32[10,4,16,128]{3,2,1,0:T(8,128)S(1)} %get-tuple-element.7.p, f32[3,16,128]{2,1,0:T(8,128)S(1)} %get-tuple-element.8.s), custom_call_target="tpu_custom_call" | custom-call | tf_op jit(solution)/shard_map/pallas_call | solution.py:491

commit v3 on v2

--- a/solution.py
+++ b/solution.py
@@ -27,8 +27,8 @@
     B, S, ITEMS,
     tr, hd_in, vm_in, lt_in, sd_in, nb_in, baro_in,
     Y, C, out_s,
-    hd, vm, lt, sd, nb, baro, X, TOPS, BOTS, HA, HB, CP, CR, TOT, TIN, M, NBI, G, E, D, AP, T, BT, PA, PB, QA, QB,
-    loc, lev_sem, bot_s, bot_r, top_s, top_r, col_s, col_r, m_s, m_r, g_s, g_r, core_s, core_r,
+    hd, vm, lt, sd, nb, baro, X, TOPS, BOTS, HA, HB, CP, CR, TOT, TIN, M, NBI, G, D, AP, T, BT, PA, PB, QA, QB,
+    loc, lev_sem, bot_s, bot_r, top_s, top_r, col_s, col_r, m_s, m_r, g_s, g_r, gc_s, gc_r, core_s, core_r,
 ):
     L, NBD, RC, CC = ITEMS
     BS = B * S
@@ -109,15 +109,6 @@
             X[t, outer, b] = zero_block
 
     load.wait()
-    pl.semaphore_wait(barrier, BS)
-
-    level_copy = remote(
-        tr.at[:, pl.ds(other * (L - 1), 1)],
-        X.at[:, pl.ds(lev * (L + 1), 1)],
-        lev_sem.at[0], lev_sem.at[1], to_core,
-    )
-    level_copy.start()
-
     my_top = sub
     my_bot = S + sub
 
@@ -134,9 +125,18 @@
             last = jnp.where(mine, pltpu.roll(X[t, k + 1, NBD - 1], 2 * spot + 1, 1), last)
         return first, last
 
-    first, last = lax.fori_loop(0, L, pack, (zero_block, zero_block))
+    many = 5 if L % 5 == 0 else 1
+
+    def pack_many(i, packed):
+        for j in range(many):
+            packed = pack(i * many + j, packed)
+        return packed
+
+    first, last = lax.fori_loop(0, L // many, pack_many, (zero_block, zero_block))
     CP[0] = first
     CP[1] = last
+
+    pl.semaphore_wait(barrier, BS)
 
     def top_slot(i):
         return TOPS.at[i]
@@ -175,6 +175,13 @@
     each_edge(lambda c: c.start())
     pl.when(me > 0)(lambda: col_down().start())
     pl.when(me < BS - 1)(lambda: col_up().start())
+
+    level_copy = remote(
+        tr.at[:, pl.ds(other * (L - 1), 1)],
+        X.at[:, pl.ds(lev * (L + 1), 1)],
+        lev_sem.at[0], lev_sem.at[1], to_core,
+    )
+    level_copy.start()
 
     def m_to(d):
         dev = (me + d) % BS
@@ -267,16 +274,9 @@
     tot_copy = remote(TOT, TIN, core_s.at[0], core_r.at[0], to_core)
     tot_copy.start()
 
-    @pl.loop(1, BS)
-    def _(d):
-        m_from(d).wait_recv()
-
-    m_core = remote(M.at[:, lev], M.at[:, lev], core_s.at[1], core_r.at[1], to_core)
-    m_core.start()
-
     tot_copy.wait_recv()
-    for j in range(H):
-        G[me, lev, j] = TOT[lev * H + j] + TIN[lev * H + j]
+    for b in range(NBD):
+        G[me, b // H, b % H] = TOT[b] + TIN[b]
 
     def g_to(d):
         dev = (me + d) % BS
@@ -289,6 +289,13 @@
     @pl.loop(1, BS)
     def _(d):
         g_to(d).start()
+
+    @pl.loop(1, BS)
+    def _(d):
+        m_from(d).wait_recv()
+
+    m_core = remote(M.at[:, lev], M.at[:, lev], core_s.at[1], core_r.at[1], to_core)
+    m_core.start()
 
     remote(M.at[:, other], M.at[:, other], core_s.at[1], core_r.at[1], to_core).wait_recv()
 
@@ -312,29 +319,38 @@
     D[0] = zero_block
     D[NR + 1] = zero_block
 
+    def over_core(d, l):
+        dev = (me + d) % BS
+        return remote(G.at[dev, l], G.at[dev, l], gc_s.at[dev], gc_r.at[dev], to_core)
+
     @pl.loop(1, BS)
     def _(d):
         g_from(d).wait_recv()
-
-    g_core = remote(G.at[:, lev], G.at[:, lev], core_s.at[2], core_r.at[2], to_core)
-    g_core.start()
-    remote(G.at[:, other], G.at[:, other], core_s.at[2], core_r.at[2], to_core).wait_recv()
-    g_core.wait_send()
+        over_core(d, lev).start()
+
+    @pl.loop(1, BS)
+    def _(d):
+        over_core(d, other).wait_recv()
 
     @pl.loop(1, BS)
     def _(d):
         g_to(d).wait_send()
+        over_core(d, lev).wait_send()
 
     def total(acc):
         return jnp.sum(jnp.sum(acc, axis=0, keepdims=True), axis=1, keepdims=True)
 
     def over_blocks(body, carry):
-        def devs(d, carry):
-            for b in range(NBD):
-                carry = body(d, b, d * NBD + b, carry)
+        pair = 2 if BS % 2 == 0 else 1
+
+        def devs(i, carry):
+            for p in range(pair):
+                d = i * pair + p
+                for b in range(NBD):
+                    carry = body(d, b, d * NBD + b, carry)
             return carry
 
-        return lax.fori_loop(0, BS, devs, carry)
+        return lax.fori_loop(0, BS // pair, devs, carry)
 
     def set_direction(q, d):
         D[q + 1] = d
@@ -344,17 +360,18 @@
     def begin(d, b, q, acc):
         f = G[d, b // H, b % H]
         set_direction(q, f)
-        E[q] = zero_block
         return acc + f * f
 
     norm_now = total(over_blocks(begin, zero_block))
+    wanted = [me * NBD + b for b in range(NBD)]
+    wanted += [jnp.maximum(baro[s], 0) for s in range(baro.shape[0])]
+    eta = [zero_block] * len(wanted)
     for iteration in range(ITERS):
         tops, bots = T[...], BT[...]
         up_rows = jnp.dot(QA[...], bots, precision=HIGH, preferred_element_type=F32)
         down_rows = jnp.dot(QB[...], tops, precision=HIGH, preferred_element_type=F32)
         HA2 = jnp.where(PA[...] < 0, T[0:NR, :], up_rows)
         HB2 = jnp.where(PB[...] < 0, BT[0:NR, :], down_rows)
-        AP[NR] = zero_block
         T[0:NR, :] = HA2
         BT[0:NR, :] = HB2
 
@@ -372,19 +389,15 @@
 
         size = norm_now / total(over_blocks(apply, zero_block))
 
+        eta = [e + size * D[q + 1] for e, q in zip(eta, wanted)]
+        if iteration == ITERS - 1:
+            break
+
         def update(d, b, q, acc):
-            E[q] = E[q] + size * D[q + 1]
             r = G[d, b // H, b % H] - size * AP[q]
             G[d, b // H, b % H] = r
             return acc + r * r
 
-        if iteration == ITERS - 1:
-            def finish(d, b, q, acc):
-                E[q] = E[q] + size * D[q + 1]
-                return acc
-
-            over_blocks(finish, jnp.int32(0))
-            break
         norm_next = total(over_blocks(update, zero_block))
         beta = norm_next / norm_now
 
@@ -396,17 +409,17 @@
         norm_now = norm_next
 
     levf = lev.astype(F32)
-    eta = [E[me * NBD + b] - levf * TIN[b] for b in range(NBD)]
+    raised = [eta[b] - levf * TIN[b] for b in range(NBD)]
 
     def press(k, _):
         for b in range(NBD):
-            C[k, b] = eta[b] - C[k, b]
+            C[k, b] = raised[b] - C[k, b]
         return 0
 
     lax.fori_loop(0, L, press, 0)
     for s in range(baro.shape[0]):
         held = baro[s]
-        out_s[s] = jnp.where(jnp.full((RC, CC), held, jnp.int32) >= 0, E[jnp.maximum(held, 0)], 0.0)
+        out_s[s] = jnp.where(jnp.full((RC, CC), held, jnp.int32) >= 0, eta[NBD + s], 0.0)
 
     level_copy.wait_send()
     each_edge(lambda c: c.wait_send())
@@ -452,9 +465,8 @@
         vm((BS, 2, H * RC + H * 4, CC), F32),
         vm((NR * 4, CC), jnp.int32),
         vm((BS, 2, H, RC, CC), F32),
+        vm((NR + 2, RC, CC), F32),
         vm((NR, RC, CC), F32),
-        vm((NR + 2, RC, CC), F32),
-        vm((NR + 1, RC, CC), F32),
         vm((KP, CC), F32),
         vm((KP, CC), F32),
         vm((NR, CC), jnp.int32),
@@ -462,7 +474,7 @@
         vm((NR, KP), F32),
         vm((NR, KP), F32),
         dma((7,)), dma((2,)), dma((2 * S,)), dma((2 * S,)), dma((2 * S,)), dma((2 * S,)),
-        dma((2,)), dma((2,)), dma((BS,)), dma((BS,)), dma((BS,)), dma((BS,)), dma((3,)), dma((3,)),
+        dma((2,)), dma((2,)), dma((BS,)), dma((BS,)), dma((BS,)), dma((BS,)), dma((BS,)), dma((BS,)), dma((2,)), dma((2,)),
     ]
     need = (10 * L * NBD + 7 * NR) * RC * CC * 4 + 4 * NR * KP * 4 + (8 << 20)
     vmem = pl.BlockSpec(memory_space=pltpu.VMEM)

time: 26.5 us -> 24.4 us (0.921)
  Pallas kernels: 25.7 us -> 23.6 us
    pallas_call x1, Pallas kernels: 24.8 us -> 22.6 us  [local(): pl.pallas_call(functools.partial(kernel, B, S, (L, NBD, RC, CC)), out_sha...]
where the time goes in v3:
time: 24.4 us; the launch traced here: 24.3 us
  Pallas kernels  23.6 us (97%)
  between operations  0.64 us (3%)
    pallas_call x1, Pallas kernels, local(): pl.pallas_call(functools.partial(kernel, B, S, (L, NBD, RC, CC)), out_sha...  22.6 us
    pallas_call x1, Pallas kernels, local(): pl.pallas_call(write_out, out_shape=shapes, in_specs=[vmem] * 3, out_spec...  0.98 us

profile of v3, /device:TPU:0, one launch (start us, length us, event | category | flops | bytes accessed | tf_op | source)
XLA Modules:
  0.0 24.3 jit_solution(13767746369448303197)
XLA Ops:
  0.6 22.6 %shard_map.94 = (f32[2,10,4,16,128]{4,3,2,1,0:T(8,128)S(1)}, f32[10,4,16,128]{3,2,1,0:T(8,128)S(1)}, f32[3,16,128]{2,1,0:T(8,128)S(1)}) custom-call(f32[2,10,4,16,128]{4,3,2,1,0:T(8,128)} %tr.1, f32[4,16,128]{2,1,0:T(8,128)} %hd_in.1, f32[19]{0:T(128)} %vm_in.1, f32[20]{0:T(128)} %lt_in.1, f32[4,16,128]{2,1,0:T(8,128)} %sd_in.1, s32[4,4]{1,0:T(4,128)} %nb_in.1, ...), custom_call_target="tpu_custom_call" | custom-call | tf_op jit(solution)/shard_map/pallas_call | solution.py:487
  23.3 1.0 %shard_map.95 = (f32[2,10,4,16,128]{4,3,2,1,0:T(8,128)}, f32[10,4,16,128]{3,2,1,0:T(8,128)}, f32[3,16,128]{2,1,0:T(8,128)}) custom-call(f32[2,10,4,16,128]{4,3,2,1,0:T(8,128)S(1)} %get-tuple-element.6.tr, f32[10,4,16,128]{3,2,1,0:T(8,128)S(1)} %get-tuple-element.7.p, f32[3,16,128]{2,1,0:T(8,128)S(1)} %get-tuple-element.8.s), custom_call_target="tpu_custom_call" | custom-call | tf_op jit(solution)/shard_map/pallas_call | solution.py:503

commit v4 on v3

--- a/solution.py
+++ b/solution.py
@@ -183,17 +183,35 @@
     )
     level_copy.start()
 
-    def m_to(d):
-        dev = (me + d) % BS
-        return remote(M.at[me, lev], M.at[me, lev], m_s.at[dev], m_r.at[me], at_dev(dev))
-
-    def m_from(d):
-        dev = (me + d) % BS
-        return remote(M.at[dev, lev], M.at[dev, lev], m_s.at[dev], m_r.at[dev], at_dev(dev))
-
-    @pl.loop(1, BS)
-    def _(d):
-        m_to(d).start()
+    def pass_piece(buf, send, recv, p, target):
+        return remote(buf.at[p, lev], buf.at[p, lev], send.at[target], recv.at[p], at_dev(target))
+
+    def along_blk(buf, send, recv, e):
+        target = ((blk + e) % B) * S + sub
+        return pass_piece(buf, send, recv, me, target)
+
+    def along_sub(buf, send, recv, e, f):
+        other_blk = (blk + e) % B
+        u = (sub + f) % S
+        p = other_blk * S + sub
+        return remote(
+            buf.at[p, lev], buf.at[p, lev], send.at[other_blk * S + u], recv.at[p],
+            at_dev(blk * S + u),
+        )
+
+    def arrive(buf, send, recv, e, f):
+        p = ((blk + e) % B) * S + (sub + f) % S
+        remote(buf.at[p, lev], buf.at[p, lev], send.at[p], recv.at[p], to_core).wait_recv()
+
+    def each_sub(act):
+        for f in range(1, S):
+            act(f)
+
+    @pl.loop(1, B)
+    def _(e):
+        along_blk(M, m_s, m_r, e).start()
+
+    each_sub(lambda f: along_sub(M, m_s, m_r, 0, f).start())
 
     n8 = lax.broadcasted_iota(jnp.int32, (R8, 2 * S * R8), 0)
     c8 = lax.broadcasted_iota(jnp.int32, (R8, 2 * S * R8), 1)
@@ -274,28 +292,38 @@
     tot_copy = remote(TOT, TIN, core_s.at[0], core_r.at[0], to_core)
     tot_copy.start()
 
+    @pl.loop(1, B)
+    def _(e):
+        arrive(M, m_s, m_r, e, 0)
+        each_sub(lambda f: along_sub(M, m_s, m_r, e, f).start())
+
+
     tot_copy.wait_recv()
     for b in range(NBD):
         G[me, b // H, b % H] = TOT[b] + TIN[b]
 
-    def g_to(d):
-        dev = (me + d) % BS
-        return remote(G.at[me, lev], G.at[me, lev], g_s.at[dev], g_r.at[me], at_dev(dev))
-
-    def g_from(d):
-        dev = (me + d) % BS
-        return remote(G.at[dev, lev], G.at[dev, lev], g_s.at[dev], g_r.at[dev], at_dev(dev))
-
-    @pl.loop(1, BS)
-    def _(d):
-        g_to(d).start()
-
-    @pl.loop(1, BS)
-    def _(d):
-        m_from(d).wait_recv()
+    def over_core(e, f, l):
+        p = ((blk + e) % B) * S + (sub + f) % S
+        return remote(G.at[p, l], G.at[p, l], gc_s.at[p], gc_r.at[p], to_core)
+
+    @pl.loop(1, B)
+    def _(e):
+        along_blk(G, g_s, g_r, e).start()
+
+    each_sub(lambda f: along_sub(G, g_s, g_r, 0, f).start())
+
+    @pl.loop(0, B)
+    def _(e):
+        each_sub(lambda f: arrive(M, m_s, m_r, e, f))
 
     m_core = remote(M.at[:, lev], M.at[:, lev], core_s.at[1], core_r.at[1], to_core)
     m_core.start()
+
+    @pl.loop(1, B)
+    def _(e):
+        arrive(G, g_s, g_r, e, 0)
+        each_sub(lambda f: along_sub(G, g_s, g_r, e, f).start())
+        over_core(e, 0, lev).start()
 
     remote(M.at[:, other], M.at[:, other], core_s.at[1], core_r.at[1], to_core).wait_recv()
 
@@ -319,23 +347,29 @@
     D[0] = zero_block
     D[NR + 1] = zero_block
 
-    def over_core(d, l):
-        dev = (me + d) % BS
-        return remote(G.at[dev, l], G.at[dev, l], gc_s.at[dev], gc_r.at[dev], to_core)
+    @pl.loop(0, B)
+    def _(e):
+        def take(f):
+            arrive(G, g_s, g_r, e, f)
+            over_core(e, f, lev).start()
+
+        each_sub(take)
 
     @pl.loop(1, BS)
     def _(d):
-        g_from(d).wait_recv()
-        over_core(d, lev).start()
+        over_core(d // S, d % S, other).wait_recv()
+
+    @pl.loop(1, B)
+    def _(e):
+        along_blk(G, g_s, g_r, e).wait_send()
+
+    @pl.loop(0, B)
+    def _(e):
+        each_sub(lambda f: along_sub(G, g_s, g_r, e, f).wait_send())
 
     @pl.loop(1, BS)
     def _(d):
-        over_core(d, other).wait_recv()
-
-    @pl.loop(1, BS)
-    def _(d):
-        g_to(d).wait_send()
-        over_core(d, lev).wait_send()
+        over_core(d // S, d % S, lev).wait_send()
 
     def total(acc):
         return jnp.sum(jnp.sum(acc, axis=0, keepdims=True), axis=1, keepdims=True)
@@ -426,9 +460,13 @@
     pl.when(me > 0)(lambda: col_down().wait_send())
     pl.when(me < BS - 1)(lambda: col_up().wait_send())
 
-    @pl.loop(1, BS)
-    def _(d):
-        m_to(d).wait_send()
+    @pl.loop(1, B)
+    def _(e):
+        along_blk(M, m_s, m_r, e).wait_send()
+
+    @pl.loop(0, B)
+    def _(e):
+        each_sub(lambda f: along_sub(M, m_s, m_r, e, f).wait_send())
 
     tot_copy.wait_send()
     m_core.wait_send()

time: 24.4 us -> 25.4 us (1.041)
  Pallas kernels: 23.6 us -> 24.6 us
    pallas_call x1, Pallas kernels: 22.6 us -> 23.7 us  [local(): pl.pallas_call(functools.partial(kernel, B, S, (L, NBD, RC, CC)), out_sha...]
where the time goes in v4:
time: 25.4 us; the launch traced here: 25.3 us
  Pallas kernels  24.6 us (97%)
  between operations  0.64 us (3%)
    pallas_call x1, Pallas kernels, local(): pl.pallas_call(functools.partial(kernel, B, S, (L, NBD, RC, CC)), out_sha...  23.7 us
    pallas_call x1, Pallas kernels, local(): pl.pallas_call(write_out, out_shape=shapes, in_specs=[vmem] * 3, out_spec...  0.98 us

profile of v4, /device:TPU:0, one launch (start us, length us, event | category | flops | bytes accessed | tf_op | source)
XLA Modules:
  0.0 25.3 jit_solution(5869435816179977141)
XLA Ops:
  0.6 23.7 %shard_map.94 = (f32[2,10,4,16,128]{4,3,2,1,0:T(8,128)S(1)}, f32[10,4,16,128]{3,2,1,0:T(8,128)S(1)}, f32[3,16,128]{2,1,0:T(8,128)S(1)}) custom-call(f32[2,10,4,16,128]{4,3,2,1,0:T(8,128)} %tr.1, f32[4,16,128]{2,1,0:T(8,128)} %hd_in.1, f32[19]{0:T(128)} %vm_in.1, f32[20]{0:T(128)} %lt_in.1, f32[4,16,128]{2,1,0:T(8,128)} %sd_in.1, s32[4,4]{1,0:T(4,128)} %nb_in.1, ...), custom_call_target="tpu_custom_call" | custom-call | tf_op jit(solution)/shard_map/pallas_call | solution.py:525
  24.3 1.0 %shard_map.95 = (f32[2,10,4,16,128]{4,3,2,1,0:T(8,128)}, f32[10,4,16,128]{3,2,1,0:T(8,128)}, f32[3,16,128]{2,1,0:T(8,128)}) custom-call(f32[2,10,4,16,128]{4,3,2,1,0:T(8,128)S(1)} %get-tuple-element.6.tr, f32[10,4,16,128]{3,2,1,0:T(8,128)S(1)} %get-tuple-element.7.p, f32[3,16,128]{2,1,0:T(8,128)S(1)} %get-tuple-element.8.s), custom_call_target="tpu_custom_call" | custom-call | tf_op jit(solution)/shard_map/pallas_call | solution.py:541

commit v5 on v3

--- a/solution.py
+++ b/solution.py
@@ -268,7 +268,14 @@
             new.append(col)
         return tuple(new)
 
-    totals = lax.fori_loop(0, L, step, (zero_block,) * NBD)
+    twice = 2 if L % 2 == 0 else 1
+
+    def step_more(i, cols):
+        for j in range(twice):
+            cols = step(i * twice + j, cols)
+        return cols
+
+    totals = lax.fori_loop(0, L // twice, step_more, (zero_block,) * NBD)
     for b in range(NBD):
         TOT[b] = totals[b]
     tot_copy = remote(TOT, TIN, core_s.at[0], core_r.at[0], to_core)
@@ -341,7 +348,7 @@
         return jnp.sum(jnp.sum(acc, axis=0, keepdims=True), axis=1, keepdims=True)
 
     def over_blocks(body, carry):
-        pair = 2 if BS % 2 == 0 else 1
+        pair = 4 if BS % 4 == 0 else 1
 
         def devs(i, carry):
             for p in range(pair):

time: 24.4 us -> 23.3 us (0.955)
  Pallas kernels: 23.6 us -> 22.5 us
    pallas_call x1, Pallas kernels: 22.6 us -> 21.5 us  [local(): pl.pallas_call(functools.partial(kernel, B, S, (L, NBD, RC, CC)), out_sha...]
where the time goes in v5:
time: 23.3 us; the launch traced here: 23.1 us
  Pallas kernels  22.5 us (97%)
  between operations  0.64 us (3%)
    pallas_call x1, Pallas kernels, local(): pl.pallas_call(functools.partial(kernel, B, S, (L, NBD, RC, CC)), out_sha...  21.5 us
    pallas_call x1, Pallas kernels, local(): pl.pallas_call(write_out, out_shape=shapes, in_specs=[vmem] * 3, out_spec...  0.98 us

profile of v5, /device:TPU:0, one launch (start us, length us, event | category | flops | bytes accessed | tf_op | source)
XLA Modules:
  0.0 23.1 jit_solution(1924783727371898522)
XLA Ops:
  0.6 21.5 %shard_map.94 = (f32[2,10,4,16,128]{4,3,2,1,0:T(8,128)S(1)}, f32[10,4,16,128]{3,2,1,0:T(8,128)S(1)}, f32[3,16,128]{2,1,0:T(8,128)S(1)}) custom-call(f32[2,10,4,16,128]{4,3,2,1,0:T(8,128)} %tr.1, f32[4,16,128]{2,1,0:T(8,128)} %hd_in.1, f32[19]{0:T(128)} %vm_in.1, f32[20]{0:T(128)} %lt_in.1, f32[4,16,128]{2,1,0:T(8,128)} %sd_in.1, s32[4,4]{1,0:T(4,128)} %nb_in.1, ...), custom_call_target="tpu_custom_call" | custom-call | tf_op jit(solution)/shard_map/pallas_call | solution.py:494
  22.1 1.0 %shard_map.95 = (f32[2,10,4,16,128]{4,3,2,1,0:T(8,128)}, f32[10,4,16,128]{3,2,1,0:T(8,128)}, f32[3,16,128]{2,1,0:T(8,128)}) custom-call(f32[2,10,4,16,128]{4,3,2,1,0:T(8,128)S(1)} %get-tuple-element.6.tr, f32[10,4,16,128]{3,2,1,0:T(8,128)S(1)} %get-tuple-element.7.p, f32[3,16,128]{2,1,0:T(8,128)S(1)} %get-tuple-element.8.s), custom_call_target="tpu_custom_call" | custom-call | tf_op jit(solution)/shard_map/pallas_call | solution.py:510
